TPU v7x, 512 devices: a whole 4x4x16 slice. The times are simulated.
512 devices in a mesh: section: 16 (over z), seq: 32 (over x, y, core).
Axes of the slice: x: 4, y: 4, z: 16, core: 2. Of those that a mesh axis runs over, the one named last changes fastest.
Arguments:
- pre_act: bfloat16 [16, 8192, 4096], P('section', 'seq'), may hold values from -6 to 6
- out_grad: bfloat16 [16, 8192, 1024], P('section', 'seq'), may hold values from -6 to 6
- proj_weight: bfloat16 [16, 1024, 4096], P('section', 'seq'), may hold values from -0.1875 to 0.1875
- lengths: int32 [16, 32], P('section'), may hold values from 0 to 512, as said below
- link_bits: int32 [16, 32], P('section', 'seq'), may hold values 0 or 1
Outputs:
- passed: bfloat16 [16, 8192, 1024], P('section', 'seq')
Inputs may be any that keep to these rules, and one draw needn't show every extreme that they name: `lengths`: one row a section: positive entries come first, then zeros; the users they describe fill the section's 32 tiles exactly, each taking ceil(length / 256) consecutive tiles, so no history spans more than 2 tiles; the first user of every section has 512 actions.
All inputs are finite; a program needn't handle non-finite values. No bound on the sum of `link_bits` on one device may be relied on, other than what follows from the above.
Results may differ from a plain program's by a relative error of at most 0.01.
Values may be sent and summed in bfloat16 or wider, within the bound.
A program may use at most 128 MiB of HBM per device.

v0:
```python
import jax
import jax.numpy as jnp
from jax import lax
from jax.sharding import PartitionSpec as P

D = 1024
HEADS = 8
HEAD_DIM = 128
TILE = 256


EPSILON = 1e-05


def from_behind(value, axis, steps):
    count = lax.axis_size(axis)
    first, last = (max(0, -steps), min(count, count - steps))
    return lax.ppermute(value, axis, [(source, source + steps) for source in range(first, last)])


def silu_slope(values):
    sigmoid_val = jax.nn.sigmoid(values)
    return sigmoid_val * (1.0 + values * (1.0 - sigmoid_val))


def tile_facts(lengths, first_tile, tile_count):
    tile_ids = first_tile + jnp.arange(tile_count, dtype=jnp.int32)
    tile_spans = (lengths + (TILE - 1)) // TILE
    span_ends = jnp.cumsum(tile_spans)
    owner_user = jnp.sum((span_ends[None, :] <= tile_ids[:, None]).astype(jnp.int32), axis=1)
    user_pick = (
        jnp.arange(lengths.shape[0], dtype=jnp.int32)[None, :] == owner_user[:, None]
    ).astype(jnp.int32)
    starts = jnp.sum(user_pick * (span_ends - tile_spans)[None, :], axis=1)
    totals = jnp.sum(user_pick * lengths[None, :], axis=1)
    tile_place = tile_ids - starts
    valid_rows = jnp.minimum(totals - tile_place * TILE, TILE)
    return (tile_place, valid_rows)


def tile_masks(tile_place, valid_rows, link_bits):
    row_ids = jnp.arange(TILE, dtype=jnp.int32)
    row_ok = row_ids[None, :] < valid_rows[:, None]
    causal = row_ids[:, None] >= row_ids[None, :]
    same_mask = row_ok[:, :, None] & row_ok[:, None, :] & causal[None]
    linked = (tile_place >= 1) & (link_bits == 1)
    cross_mask = linked[:, None, None] & row_ok[:, :, None] & jnp.ones((1, 1, TILE), dtype=bool)
    return (
        row_ok.astype(jnp.float32),
        same_mask.astype(jnp.float32),
        cross_mask.astype(jnp.float32),
        linked,
    )


def attend_forward(queries, keys_in, values_in, mask, score_scale):
    scores = (
        jnp.einsum("tihd,tjhd->thij", queries, keys_in, preferred_element_type=jnp.float32)
        * score_scale
    )
    weights = (jax.nn.silu(scores) * mask[:, None] / TILE).astype(jnp.bfloat16)
    mixed = jnp.einsum("thij,tjhd->tihd", weights, values_in, preferred_element_type=jnp.float32)
    return (scores, weights, mixed)


def attend_backward(grad_mix, queries, keys_in, values_in, scores, weights, mask, score_scale):
    grad_val = jnp.einsum(
        "thij,tihd->tjhd", weights, grad_mix, preferred_element_type=jnp.float32
    ).astype(jnp.bfloat16)
    grad_att = jnp.einsum(
        "tihd,tjhd->thij", grad_mix, values_in, preferred_element_type=jnp.float32
    )
    grad_score = (grad_att * mask[:, None] / TILE * silu_slope(scores)).astype(jnp.bfloat16)
    grad_query = (
        jnp.einsum("thij,tjhd->tihd", grad_score, keys_in, preferred_element_type=jnp.float32)
        * score_scale
    )
    grad_key = (
        jnp.einsum("thij,tihd->tjhd", grad_score, queries, preferred_element_type=jnp.float32)
        * score_scale
    ).astype(jnp.bfloat16)
    return (grad_query, grad_val, grad_key)


def times_rows(grads, weight_rows):
    return lax.dot_general(
        grads, weight_rows, (((1,), (1,)), ((), ())), preferred_element_type=jnp.float32
    )


def body(pre_act, out_grad, proj_weight, lengths, link_bits):
    tile_count = pre_act.shape[1] // TILE
    first_tile = lax.axis_index("seq") * tile_count
    tile_place, valid_rows = tile_facts(lengths[0], first_tile, tile_count)
    row_ok, same_mask, cross_mask, linked = tile_masks(tile_place, valid_rows, link_bits[0])
    pre_tiles = pre_act[0].reshape(tile_count, TILE, 4 * D).astype(jnp.float32)
    slopes = silu_slope(pre_tiles)
    activated = jax.nn.silu(pre_tiles).astype(jnp.bfloat16)
    gate_u = activated[:, :, :D]
    values_in = activated[:, :, D : 2 * D].reshape(tile_count, TILE, HEADS, HEAD_DIM)
    queries = activated[:, :, 2 * D : 3 * D].reshape(tile_count, TILE, HEADS, HEAD_DIM)
    keys_in = activated[:, :, 3 * D :].reshape(tile_count, TILE, HEADS, HEAD_DIM)
    recv_key, recv_val = from_behind((keys_in, values_in), "seq", 1)
    key_prev = jnp.concatenate([recv_key, keys_in[:-1]], axis=0)
    val_prev = jnp.concatenate([recv_val, values_in[:-1]], axis=0)
    score_scale = HEAD_DIM ** (-0.5)
    same_scores, same_weights, same_mixed = attend_forward(
        queries, keys_in, values_in, same_mask, score_scale
    )
    cross_scores, cross_weights, cross_mixed = attend_forward(
        queries, key_prev, val_prev, cross_mask, score_scale
    )
    mixed = (same_mixed + cross_mixed).reshape(tile_count, TILE, D)
    row_mean = jnp.mean(mixed, axis=-1, keepdims=True)
    centered = mixed - row_mean
    inv_std = lax.rsqrt(jnp.mean(centered * centered, axis=-1, keepdims=True) + EPSILON)
    normed = centered * inv_std
    cotangent = out_grad[0].reshape(tile_count, TILE, D).astype(jnp.float32) * row_ok[:, :, None]
    grad_gate = cotangent * normed
    grad_norm = cotangent * gate_u.astype(jnp.float32)
    grad_mix = inv_std * (
        grad_norm
        - jnp.mean(grad_norm, axis=-1, keepdims=True)
        - normed * jnp.mean(grad_norm * normed, axis=-1, keepdims=True)
    )
    grad_mix = grad_mix.astype(jnp.bfloat16).reshape(tile_count, TILE, HEADS, HEAD_DIM)
    query_same, val_same, key_same = attend_backward(
        grad_mix, queries, keys_in, values_in, same_scores, same_weights, same_mask, score_scale
    )
    query_cross, val_cross, key_cross = attend_backward(
        grad_mix, queries, key_prev, val_prev, cross_scores, cross_weights, cross_mask, score_scale
    )
    grad_query = (query_same + query_cross).reshape(tile_count, TILE, D)
    row_total = tile_count * TILE
    back_val, back_key = from_behind((val_cross, key_cross), "seq", -1)
    val_next = jnp.concatenate([val_cross[1:], back_val], axis=0)
    key_next = jnp.concatenate([key_cross[1:], back_key], axis=0)
    grad_value = (val_same.astype(jnp.float32) + val_next.astype(jnp.float32)).reshape(
        tile_count, TILE, D
    )
    grad_key = (key_same.astype(jnp.float32) + key_next.astype(jnp.float32)).reshape(
        tile_count, TILE, D
    )
    grads = jnp.concatenate([grad_gate, grad_value, grad_query, grad_key], axis=-1) * slopes
    grads = grads.astype(jnp.bfloat16).reshape(row_total, 4 * D)
    grad_in = times_rows(grads, lax.all_gather(proj_weight[0], "seq", axis=0, tiled=True))
    grad_in = grad_in.astype(jnp.bfloat16).reshape(1, row_total, D)
    return from_behind(grad_in, "section", -1)


def solution(mesh):
    placed = (
        P("section", "seq", None),
        P("section", "seq", None),
        P("section", "seq", None),
        P("section", None),
        P("section", "seq"),
    )
    return jax.shard_map(
        body, mesh=mesh, in_specs=placed, out_specs=P("section", "seq", None), check_vma=False
    )
```

profile of v0, /device:TPU:1, one launch (start us, length us, event | category | flops | bytes accessed | tf_op | source)
XLA Modules:
  0.0 116.3 jit_solution(9083833117720639481)
XLA Ops:
  6.5 0.0 all-gather.3.cloned.1.call-start
  6.5 0.7 all-gather.3.cloned.1.call-update
  7.3 4.1 %copy.25 = bf16[1,256,4096]{1,2,0:T(8,128)(2,1)} copy(bf16[1,256,4096]{2,1,0:T(8,128)(2,1)} %param.5) | data formatting | bytes 4194304 | tf_op args[0]
  11.3 2.7 %fusion.5 = bf16[1,256,4096]{1,2,0:T(8,128)(2,1)S(1)} fusion(bf16[1,256,4096]{1,2,0:T(8,128)(2,1)} %copy.25), kind=kLoop, calls=%fused_computation.8 | loop fusion | flops 6291456 | bytes 4194304 | tf_op jit(solution)/shard_map/convert_element_type | solution.py:98
  14.1 0.0 copy-start.5
  14.1 0.9 fusion.51
  15.0 0.0 copy-start.1
  15.0 1.0 copy.28
  16.0 4.6 %collective-permute-start.1 = (bf16[1,256,8,128]{3,1,2,0:T(8,128)(2,1)}, bf16[1,256,8,128]{3,1,2,0:T(8,128)(2,1)}, u32[]{:S(2)}, u32[]{:S(2)}) collective-permute-start(bf16[1,256,8,128]{3,1,2,0:T(8,128)(2,1)} %copy.28), channel_id=1, source_target_pairs={{0,1},{1,2},{2,3},{3,4},{4,5},{5,6},{6,7},{7,8},{8,9},{9,10},{10,1... | collective-permute-start | bytes 1572872 | tf_op jit(solution)/shard_map/ppermute | solution.py:18
  20.6 1.9 %collective-permute-start = (bf16[1,256,8,128]{1,3,2,0:T(8,128)(2,1)}, bf16[1,256,8,128]{1,3,2,0:T(8,128)(2,1)}, u32[]{:S(2)}, u32[]{:S(2)}) collective-permute-start(bf16[1,256,8,128]{1,3,2,0:T(8,128)(2,1)} %bitcast.139), channel_id=1, source_target_pairs={{0,1},{1,2},{2,3},{3,4},{4,5},{5,6},{6,7},{7,8},{8,9},{9,10},{10,1... | collective-permute-start | bytes 1572872 | tf_op jit(solution)/shard_map/ppermute | solution.py:18
  22.5 0.0 copy-done.5
  22.6 0.1 copy.24
  22.6 0.1 reduce-window.4
  22.7 0.1 reduce.11
  22.8 0.7 fusion.47
  23.5 1.4 %fusion.46 = (s32[]{:T(128)}, s32[]{:T(128)}) fusion(s32[32]{0:T(128)S(1)} %reduce.11, s32[1,32]{1,0:T(1,128)S(1)} %copy-done.5, s32[]{:T(128)} %fusion.47), kind=kLoop, calls=%fused_computation.75 | loop fusion | flops 702 | bytes 268 | tf_op jit(solution)/shard_map/reduce_sum | solution.py:34
  26.1 0.1 fusion.44
  26.2 2.6 %multiply_convert_fusion.3 = (bf16[8,256,256]{2,1,0:T(8,128)(2,1)}, f32[8,256,256]{2,1,0:T(8,128)}) fusion(f32[256,256]{1,0:T(8,128)S(1)} %fusion.44, bf16[256,8,128]{0,2,1:T(8,128)(2,1)S(1)} %bitcast.135, bf16[256,8,128]{0,2,1:T(8,128)(2,1)S(1)} %bitcast.129), kind=kOutput, calls=%fused_computation.18 | convolution fusion | flops 138412032 | bytes 4456448 | tf_op jit(solution)/shard_map/tihd,tjhd->thij/dot_general | solution.py:58
  28.8 0.0 copy-done.1
  29.5 1.2 %copy.23 = bf16[1,256,1024]{1,2,0:T(8,128)(2,1)S(1)} copy(bf16[1,256,1024]{2,1,0:T(8,128)(2,1)} %param.6) | data formatting | bytes 1048576 | tf_op args[1]
  30.7 0.0 copy-start.2
  30.8 1.9 %fusion.53 = f32[8,128,256]{2,1,0:T(8,128)S(1)} fusion(bf16[256,8,128]{0,2,1:T(8,128)(2,1)} %bitcast.140, bf16[8,256,256]{2,1,0:T(8,128)(2,1)} %get-tuple-element.14), kind=kOutput, calls=%fused_computation.87 | convolution fusion | flops 134217728 | bytes 2621440 | tf_op jit(solution)/shard_map/thij,tjhd->tihd/dot_general | solution.py:62
  32.7 0.0 collective-permute-done.1
  32.7 0.0 copy-done.2
  32.7 2.0 %multiply_convert_fusion.2 = (bf16[8,256,256]{2,1,0:T(8,128)(2,1)S(1)}, f32[8,256,256]{2,1,0:T(8,128)S(1)}) fusion(f32[256]{0:T(256)S(1)} %and_convert_fusion, bf16[256,8,128]{0,2,1:T(8,128)(2,1)S(1)} %bitcast.136, bf16[1,256,8,128]{3,1,2,0:T(8,128)(2,1)} %collective-permute-done.1), kind=kOutput, calls=%fused_computation.16 | convolution fusion | flops 138412032 | bytes 4195328 | tf_op jit(solution)/shard_map/tihd,tjhd->thij/dot_general | solution.py:58
  34.7 0.0 collective-permute-done
  34.7 1.6 %fusion.52 = (f32[256]{0:T(256)S(1)}, f32[8,128,256]{2,1,0:T(8,128)S(1)}) fusion(f32[8,128,256]{2,1,0:T(8,128)S(1)} %fusion.53, bf16[8,256,256]{2,1,0:T(8,128)(2,1)S(1)} %get-tuple-element.16, bf16[1,256,8,128]{1,3,2,0:T(8,128)(2,1)} %collective-permute-done), kind=kOutput, calls=%fused_computation.86 | convolution fusion | flops 134741760 | bytes 3671040 | tf_op jit(solution)/shard_map/thij,tjhd->tihd/dot_general | solution.py:62
  36.3 0.2 fusion.35
  36.5 0.3 fusion.37
  36.8 1.4 %fusion.36 = (f32[1,256,1024]{1,2,0:T(8,128)}, bf16[1,256,1024]{1,2,0:T(8,128)(2,1)S(1)}) fusion(bf16[1,256,1024]{1,2,0:T(8,128)(2,1)S(1)} %copy.23, f32[8,128,256]{2,1,0:T(8,128)S(1)} %get-tuple-element.19, f32[256]{0:T(256)S(1)} %add_rsqrt_fusion, f32[256]{0:T(256)S(1)} %broadcast_multiply_fusion.2, f32[256]{0:T(256)S(1)} %fusion.50, ...), kind=kLoop, calls=%fused_computation.50 | loop fusion | flops 3145728 | bytes 3675136 | tf_op jit(solution)/shard_map/mul | solution.py:119
  38.2 0.3 fusion.28
  38.5 6.5 %collective-permute-start.2 = (bf16[1,256,8,128]{1,3,2,0:T(8,128)(2,1)S(1)}, bf16[1,256,8,128]{1,3,2,0:T(8,128)(2,1)S(1)}, u32[]{:S(2)}, u32[]{:S(2)}) collective-permute-start(bf16[1,256,8,128]{1,3,2,0:T(8,128)(2,1)S(1)} %fusion.28), channel_id=1, source_target_pairs={{1,0},{2,1},{3,2},{4,3},{5,4},{6,5},{7,6},{8,7},{9,8},{10,9},{11,1... | collective-permute-start | bytes 1572872 | tf_op jit(solution)/shard_map/ppermute | solution.py:18
  45.0 0.0 copy-start.6
  45.1 2.3 %multiply_convert_fusion = bf16[8,256,256]{2,1,0:T(8,128)(2,1)S(1)} fusion(f32[8,256,256]{2,1,0:T(8,128)S(1)} %get-tuple-element.17, bf16[256,8,128]{0,2,1:T(8,128)(2,1)S(1)} %bitcast.132, f32[256]{0:T(256)S(1)} %and_convert_fusion, bf16[1,256,8,128]{1,3,2,0:T(8,128)(2,1)} %collective-permute-done), kind=kOutput, calls=%fused_computation.14 | convolution fusion | flops 140509184 | bytes 4195328 | tf_op jit(solution)/shard_map/tihd,tjhd->thij/dot_general | solution.py:70
  47.4 0.0 copy-start.4
  47.4 0.3 fusion.29
  47.7 2.1 %collective-permute-start.3 = (bf16[1,256,8,128]{1,3,2,0:T(8,128)(2,1)S(1)}, bf16[1,256,8,128]{1,3,2,0:T(8,128)(2,1)S(1)}, u32[]{:S(2)}, u32[]{:S(2)}) collective-permute-start(bf16[1,256,8,128]{1,3,2,0:T(8,128)(2,1)S(1)} %fusion.29), channel_id=1, source_target_pairs={{1,0},{2,1},{3,2},{4,3},{5,4},{6,5},{7,6},{8,7},{9,8},{10,9},{11,1... | collective-permute-start | bytes 1572872 | tf_op jit(solution)/shard_map/ppermute | solution.py:18
  49.8 0.0 copy-done.6
  49.9 0.0 copy-done.4
  49.9 1.1 multiply_convert_fusion.1
  51.0 0.5 fusion.54
  51.5 0.0 copy-start.3
  51.5 2.6 %fusion.12 = f32[8,128,256]{2,1,0:T(8,128)} fusion(f32[8,128,256]{2,1,0:T(8,128)S(1)} %fusion.54, bf16[8,256,256]{2,1,0:T(8,128)(2,1)S(1)} %multiply_convert_fusion, bf16[1,256,8,128]{3,1,2,0:T(8,128)(2,1)} %collective-permute-done.1), kind=kOutput, calls=%fused_computation.23 | convolution fusion | flops 134742016 | bytes 3670016 | tf_op jit(solution)/shard_map/thij,tjhd->tihd/dot_general | solution.py:75
  54.1 0.0 collective-permute-done.2
  54.1 0.0 copy-done.3
  54.1 1.4 %convert_add_fusion.1 = f32[1,256,8,128]{1,3,2,0:T(8,128)} fusion(bf16[1,256,8,128]{1,3,2,0:T(8,128)(2,1)S(1)} %collective-permute-done.2, bf16[256,8,128]{0,2,1:T(8,128)(2,1)S(1)} %bitcast.134, bf16[8,256,256]{2,1,0:T(8,128)(2,1)S(1)} %copy-done.3), kind=kOutput, calls=%fused_computation.45 | convolution fusion | flops 135266304 | bytes 3145728 | tf_op jit(solution)/shard_map/thij,tihd->tjhd/dot_general | solution.py:67
  55.5 0.0 copy-start
  55.5 2.7 %collective-permute-done.3 = bf16[1,256,8,128]{1,3,2,0:T(8,128)(2,1)S(1)} collective-permute-done((bf16[1,256,8,128]{1,3,2,0:T(8,128)(2,1)S(1)}, bf16[1,256,8,128]{1,3,2,0:T(8,128)(2,1)S(1)}, u32[]{:S(2)}, u32[]{:S(2)}) %collective-permute-start.3) | collective-permute-done | bytes 524320 | tf_op jit(solution)/shard_map/ppermute | solution.py:18
  58.2 1.3 %convert_add_fusion = f32[1,256,8,128]{1,3,2,0:T(8,128)} fusion(bf16[1,256,8,128]{1,3,2,0:T(8,128)(2,1)S(1)} %collective-permute-done.3, bf16[256,8,128]{0,2,1:T(8,128)(2,1)S(1)} %bitcast.138, bf16[8,256,256]{2,1,0:T(8,128)(2,1)S(1)} %multiply_convert_fusion.1), kind=kOutput, calls=%fused_computation.44 | convolution fusion | flops 135528448 | bytes 3145728 | tf_op jit(solution)/shard_map/thij,tihd->tjhd/dot_general | solution.py:79
  59.5 25.8 %all-gather.3.cloned.1.call-done = bf16[1,1024,4096]{2,1,0:T(8,128)(2,1)} async-done(((bf16[1,32,4096]{2,1,0:T(8,128)(2,1)}), bf16[1,1024,4096]{2,1,0:T(8,128)(2,1)}) %all-gather.3.cloned.1.call-update) | async-done | bytes 8388624 | tf_op jit(solution)/shard_map/all_gather | solution.py:146
  85.3 0.0 copy-done
  85.3 8.2 %fusion.20 = bf16[1,256,1024]{2,1,0:T(8,128)(2,1)S(1)} fusion(bf16[1,1024,4096]{2,1,0:T(8,128)(2,1)} %all-gather.3.cloned.1.call-done, bf16[1,256,4096]{1,2,0:T(8,128)(2,1)S(1)} %copy-done, f32[1,256,1024]{1,2,0:T(8,128)} %bitcast.144, f32[1,256,1024]{1,2,0:T(8,128)} %bitcast.142, f32[1,256,1024]{1,2,0:T(8,128)} %bitcast.143, ...), kind=kOutput, calls=%fused_computation.30 | convolution fusion | flops 2161377280 | bytes 15204352 | tf_op jit(solution)/shard_map/dot_general | solution.py:86
  93.5 1.3 %collective-permute-start.4 = (bf16[1,256,1024]{2,1,0:T(8,128)(2,1)S(1)}, bf16[1,256,1024]{2,1,0:T(8,128)(2,1)S(1)}, u32[]{:S(2)}, u32[]{:S(2)}) collective-permute-start(bf16[1,256,1024]{2,1,0:T(8,128)(2,1)S(1)} %fusion.20), channel_id=1, source_target_pairs={{32,0},{64,32},{96,64},{128,96},{160,128},{192,160},{224,192},{256... | collective-permute-start | bytes 1572872 | tf_op jit(solution)/shard_map/ppermute | solution.py:18
  94.8 13.9 %collective-permute-done.4 = bf16[1,256,1024]{2,1,0:T(8,128)(2,1)S(1)} collective-permute-done((bf16[1,256,1024]{2,1,0:T(8,128)(2,1)S(1)}, bf16[1,256,1024]{2,1,0:T(8,128)(2,1)S(1)}, u32[]{:S(2)}, u32[]{:S(2)}) %collective-permute-start.4) | collective-permute-done | bytes 524320 | tf_op jit(solution)/shard_map/ppermute | solution.py:18
  108.7 0.8 copy.45
  (7 shorter events, 0.0 us)
Async XLA Ops:
  6.5 78.7 %all-gather.3.cloned.1.call-start = ((), (), s32[]{:S(2)}) async-start(), calls=%async_computation | async-start | bytes 8650752 | tf_op jit(solution)/shard_map/all_gather | solution.py:146
  14.1 8.4 %copy-start.5 = (s32[1,32]{1,0:T(1,128)S(1)}, s32[1,32]{1,0:T(1,128)}, u32[]{:S(2)}) copy-start(s32[1,32]{1,0:T(1,128)} %param.8) | copy-start | bytes 388
  15.0 13.8 %copy-start.1 = (bf16[1,256,1024]{1,2,0:T(8,128)(2,1)}, bf16[1,256,1024]{1,2,0:T(8,128)(2,1)S(1)}, u32[]{:S(2)}) copy-start(bf16[1,256,1024]{1,2,0:T(8,128)(2,1)S(1)} %get-tuple-element.11) | copy-start | bytes 1572868
  16.0 16.7 %collective-permute-start.1 = (bf16[1,256,8,128]{3,1,2,0:T(8,128)(2,1)}, bf16[1,256,8,128]{3,1,2,0:T(8,128)(2,1)}, u32[]{:S(2)}, u32[]{:S(2)}) collective-permute-start(bf16[1,256,8,128]{3,1,2,0:T(8,128)(2,1)} %copy.28), channel_id=1, source_target_pairs={{0,1},{1,2},{2,3},{3,4},{4,5},{5,6},{6,7},{7,8},{8,9},{9,10},{10,1... | collective-permute-start | bytes 1572872 | tf_op jit(solution)/shard_map/ppermute | solution.py:18
  20.6 14.1 %collective-permute-start = (bf16[1,256,8,128]{1,3,2,0:T(8,128)(2,1)}, bf16[1,256,8,128]{1,3,2,0:T(8,128)(2,1)}, u32[]{:S(2)}, u32[]{:S(2)}) collective-permute-start(bf16[1,256,8,128]{1,3,2,0:T(8,128)(2,1)} %bitcast.139), channel_id=1, source_target_pairs={{0,1},{1,2},{2,3},{3,4},{4,5},{5,6},{6,7},{7,8},{8,9},{9,10},{10,1... | collective-permute-start | bytes 1572872 | tf_op jit(solution)/shard_map/ppermute | solution.py:18
  30.7 2.0 %copy-start.2 = (bf16[1,256,1024]{1,2,0:T(8,128)(2,1)S(1)}, bf16[1,256,1024]{1,2,0:T(8,128)(2,1)}, u32[]{:S(2)}) copy-start(bf16[1,256,1024]{1,2,0:T(8,128)(2,1)} %copy-done.1) | copy-start | bytes 1572868
  38.5 15.6 %collective-permute-start.2 = (bf16[1,256,8,128]{1,3,2,0:T(8,128)(2,1)S(1)}, bf16[1,256,8,128]{1,3,2,0:T(8,128)(2,1)S(1)}, u32[]{:S(2)}, u32[]{:S(2)}) collective-permute-start(bf16[1,256,8,128]{1,3,2,0:T(8,128)(2,1)S(1)} %fusion.28), channel_id=1, source_target_pairs={{1,0},{2,1},{3,2},{4,3},{5,4},{6,5},{7,6},{8,7},{9,8},{10,9},{11,1... | collective-permute-start | bytes 1572872 | tf_op jit(solution)/shard_map/ppermute | solution.py:18
  45.0 4.8 %copy-start.6 = (f32[8,256,256]{2,1,0:T(8,128)S(1)}, f32[8,256,256]{2,1,0:T(8,128)}, u32[]{:S(2)}) copy-start(f32[8,256,256]{2,1,0:T(8,128)} %get-tuple-element.15) | copy-start | bytes 6291460
  47.4 2.5 %copy-start.4 = (bf16[1,256,1024]{1,2,0:T(8,128)(2,1)S(1)}, bf16[1,256,1024]{1,2,0:T(8,128)(2,1)}, u32[]{:S(2)}) copy-start(bf16[1,256,1024]{1,2,0:T(8,128)(2,1)} %get-tuple-element.9) | copy-start | bytes 1572868
  47.7 10.5 %collective-permute-start.3 = (bf16[1,256,8,128]{1,3,2,0:T(8,128)(2,1)S(1)}, bf16[1,256,8,128]{1,3,2,0:T(8,128)(2,1)S(1)}, u32[]{:S(2)}, u32[]{:S(2)}) collective-permute-start(bf16[1,256,8,128]{1,3,2,0:T(8,128)(2,1)S(1)} %fusion.29), channel_id=1, source_target_pairs={{1,0},{2,1},{3,2},{4,3},{5,4},{6,5},{7,6},{8,7},{9,8},{10,9},{11,1... | collective-permute-start | bytes 1572872 | tf_op jit(solution)/shard_map/ppermute | solution.py:18
  51.5 2.6 %copy-start.3 = (bf16[8,256,256]{2,1,0:T(8,128)(2,1)S(1)}, bf16[8,256,256]{2,1,0:T(8,128)(2,1)}, u32[]{:S(2)}) copy-start(bf16[8,256,256]{2,1,0:T(8,128)(2,1)} %get-tuple-element.14) | copy-start | bytes 3145732
  55.5 29.8 %copy-start = (bf16[1,256,4096]{1,2,0:T(8,128)(2,1)S(1)}, bf16[1,256,4096]{1,2,0:T(8,128)(2,1)}, u32[]{:S(2)}) copy-start(bf16[1,256,4096]{1,2,0:T(8,128)(2,1)} %copy.25) | copy-start | bytes 6291460
  93.5 15.2 %collective-permute-start.4 = (bf16[1,256,1024]{2,1,0:T(8,128)(2,1)S(1)}, bf16[1,256,1024]{2,1,0:T(8,128)(2,1)S(1)}, u32[]{:S(2)}, u32[]{:S(2)}) collective-permute-start(bf16[1,256,1024]{2,1,0:T(8,128)(2,1)S(1)} %fusion.20), channel_id=1, source_target_pairs={{32,0},{64,32},{96,64},{128,96},{160,128},{192,160},{224,192},{256... | collective-permute-start | bytes 1572872 | tf_op jit(solution)/shard_map/ppermute | solution.py:18
Sparse Core Ops, SparseCore 0:
  10.5 74.7 all-gather.2
where the time goes:
time: 117 us; the launch traced here: 116 us
  waiting for transfers between devices  43.1 us (37%)
  matrix products  26.1 us (22%)
  starting transfers between devices  16.4 us (14%)
  between operations  15.5 us (13%)
  local copies, waits for them, and re-layouts  8.13 us (7%)
  other arithmetic  7.04 us (6%)
    all_gather x1, waiting for transfers between devices, body(): lax.all_gather(proj_weight[0], 'seq', axis=0, tiled=True)  25.8 us
    ppermute x5, waiting for transfers between devices, from_behind(): lax.ppermute(value, axis, [(source, source + steps) for source in range(f...  16.6 us
    ppermute x5, starting transfers between devices, from_behind(): lax.ppermute(value, axis, [(source, source + steps) for source in range(f...  16.4 us
    dot_general x1, matrix products, times_rows(): lax.dot_general(grads, weight_rows, (((1,), (1,)), ((), ())), preferred_e...  8.23 us
    unnamed x17, local copies, waits for them, and re-layouts  6.15 us
    dot_general x2, matrix products, attend_forward(): jnp.einsum('tihd,tjhd->thij', queries, keys_in, preferred_element_type=jn...  4.56 us
    dot_general x2, matrix products, attend_backward(): jnp.einsum('tihd,tjhd->thij', grad_mix, values_in, preferred_element_type...  3.48 us
    dot_general x2, matrix products, attend_forward(): jnp.einsum('thij,tjhd->tihd', weights, values_in, preferred_element_type=...  3.47 us
  transfers between devices with their start and end apart: 6, of which 3 were waited for; matrix products, arithmetic and copies ran while one was open for 28% of the time, Pallas kernels for 0%

commit v1 on v0

v1 whole, which is shorter than its diff:
```python
import jax
import jax.numpy as jnp
from jax import lax
from jax.experimental import pallas as pl
from jax.experimental.pallas import tpu as pltpu
from jax.sharding import PartitionSpec as P

D = 1024
HEADS = 8
HEAD_DIM = 128
TILE = 256
SIDE = 4
SECTIONS = 16
DEVICES = 32
SHARD = D // DEVICES
EPSILON = 1e-05
MESH = pl.DeviceIdType.MESH
F32 = jnp.float32
BF16 = jnp.bfloat16
SCALE = HEAD_DIM ** (-0.5)

PIECE = 256
PIECES = D // PIECE

A_FROM = {-1: 0, 1: 1}
A_FAR = (2, 3)
LANES = (0, -1, 1, 2)
B_FROM = {(a, s): 4 + 4 * i + j for i, a in enumerate(LANES) for j, s in enumerate((-1, 1))}
B_FAR = {(a, h): 4 + 4 * i + 2 + h for i, a in enumerate(LANES) for h in range(2)}
SWAP = {(a, b): 20 + 4 * i + j for i, a in enumerate(LANES) for j, b in enumerate(LANES)}
K_IN = 36
V_IN = 40
Q_IN = 44
DO_IN = 48
OUT = 52
TRANSFERS = 56


def mod(value, size):
    return lax.rem(value + size, size)


def dot_nn(a, b):
    return lax.dot_general(a, b, (((1,), (0,)), ((), ())), preferred_element_type=F32)


def dot_nt(a, b):
    return lax.dot_general(a, b, (((1,), (1,)), ((), ())), preferred_element_type=F32)


def dot_tn(a, b):
    return lax.dot_general(a, b, (((0,), (0,)), ((), ())), preferred_element_type=F32)


def sigmoid(values):
    return 0.5 * jnp.tanh(0.5 * values) + 0.5


def kernel(
    len_ref, link_ref, pre, og, w, out,
    pre_v, og_v, wbuf, kraw, vraw, qraw, doraw, kbuf, vbuf, qbuf, dobuf, gate_buf, slopes,
    p_same, s_same, p_cross, s_cross, mix, grads, staged,
    send_sem, recv_sem, local_sem,
):
    section = lax.axis_index("section")
    me = lax.axis_index("seq")
    core = lax.rem(me, 2)
    cy = lax.rem(lax.div(me, 2), SIDE)
    cx = lax.div(me, 2 * SIDE)
    other = me + 1 - 2 * core
    after = mod(me + 1, DEVICES)
    before = mod(me - 1, DEVICES)

    def at(a, b, c=None):
        c = core if c is None else c
        x = mod(cx + a * (1 - c) + b * c, SIDE)
        y = mod(cy + a * c + b * (1 - c), SIDE)
        return (x * SIDE + y) * 2 + c

    def rows(device, half=None):
        if half is None:
            return pl.ds(pl.multiple_of(device * SHARD, SHARD), SHARD)
        size = SHARD // 2
        return pl.ds(pl.multiple_of(device * SHARD + half * size, size), size)

    barrier = pltpu.get_barrier_semaphore()
    peers = [
        {"seq": other},
        {"seq": at(1, 0)},
        {"seq": at(-1, 0)},
        {"seq": at(0, 1)},
        {"seq": at(0, -1)},
        {"seq": after + (before - after) * (1 - core)},
        {"section": mod(section + 1, SECTIONS)},
        {"section": mod(section - 1, SECTIONS)},
    ]

    local = [
        pltpu.make_async_copy(pre.at[0, :, pl.ds(D * i, D)], pre_v.at[:, pl.ds(D * i, D)], local_sem.at[i])
        for i in range(4)
    ]
    local.append(pltpu.make_async_copy(og.at[0], og_v, local_sem.at[4]))
    local.append(pltpu.make_async_copy(w.at[0], wbuf.at[rows(me)], local_sem.at[5]))
    for i in (3, 1, 2, 0, 4, 5):
        local[i].start()
    for peer in peers:
        pl.semaphore_signal(barrier, inc=1, device_id=peer, device_id_type=MESH)
    pl.semaphore_wait(barrier, len(peers))

    sent = []

    def copy(src, dst, number, target):
        return pltpu.make_async_remote_copy(
            src_ref=src, dst_ref=dst, send_sem=send_sem.at[number], recv_sem=recv_sem.at[number],
            device_id=target, device_id_type=MESH,
        )

    def send(src, dst, number, target):
        moved = copy(src, dst, number, {"seq": target})
        moved.start()
        sent.append(moved)

    def arrived(dst, number):
        copy(dst, dst, number, {"seq": other}).wait_recv()

    def columns(i):
        return pl.ds(PIECE * i, PIECE)

    for i in range(PIECES):
        send(pre.at[0, :, pl.ds(3 * D + PIECE * i, PIECE)], kraw.at[:, columns(i)], K_IN + i, after)
        send(pre.at[0, :, pl.ds(D + PIECE * i, PIECE)], vraw.at[:, columns(i)], V_IN + i, after)
        send(pre.at[0, :, pl.ds(2 * D + PIECE * i, PIECE)], qraw.at[:, columns(i)], Q_IN + i, before)

    def block(device, half=None):
        return wbuf.at[rows(device, half)]

    def pass_on(src, a, b):
        send(src, block(at(a, b)), SWAP[a, b], other)

    def spread(src, a):
        send(src, block(at(a, 0)), B_FROM[a, -1], at(0, 1))
        send(src, block(at(a, 0)), B_FROM[a, 1], at(0, -1))
        pass_on(src, a, 0)

    def own_out():
        send(w.at[0], block(me), A_FROM[-1], at(1, 0))
        send(w.at[0], block(me), A_FROM[1], at(-1, 0))
        spread(w.at[0], 0)

    def first_axis():
        arrived(block(at(-1, 0)), A_FROM[-1])
        send(block(at(-1, 0), 0), block(at(-1, 0), 0), A_FAR[0], at(1, 0))
        arrived(block(at(1, 0)), A_FROM[1])
        send(block(at(1, 0), 1), block(at(1, 0), 1), A_FAR[1], at(-1, 0))
        spread(block(at(-1, 0)), -1)
        spread(block(at(1, 0)), 1)

    def first_axis_far():
        for half in range(2):
            arrived(block(at(2, 0), half), A_FAR[half])
        spread(block(at(2, 0)), 2)

    def second_axis(a):
        for half, step in enumerate((-1, 1)):
            arrived(block(at(a, step)), B_FROM[a, step])
            send(block(at(a, step), half), block(at(a, step), half), B_FAR[a, half], at(0, -step))
            pass_on(block(at(a, step)), a, step)

    def second_axis_far(a):
        for half in range(2):
            arrived(block(at(a, 2), half), B_FAR[a, half])
        pass_on(block(at(a, 2)), a, 2)

    def swapped(a, b):
        arrived(block(at(a, b, 1 - core)), SWAP[a, b])

    own_out()

    end = jnp.int32(0)
    place = jnp.int32(0)
    total = jnp.int32(0)
    for user in range(DEVICES):
        length = len_ref[0, user]
        begin = end
        end = begin + lax.div(length + (TILE - 1), TILE)
        mine = jnp.logical_and(begin <= me, me < end)
        place = jnp.where(mine, me - begin, place)
        total = jnp.where(mine, length, total)
    valid = jnp.minimum(total - place * TILE, TILE)
    linked = jnp.where(jnp.logical_and(place >= 1, link_ref[0, 0] == 1), 1, 0).astype(jnp.int32)
    takes = linked.astype(F32)
    gives = 1.0 - takes

    def activate(group, target):
        def step(i, carry):
            at_rows = pl.ds(pl.multiple_of(i * 32, 32), 32)
            value = pre_v[at_rows, pl.ds(D * group, D)].astype(F32)
            s = sigmoid(value)
            act = value * s
            target[at_rows, :] = act.astype(BF16)
            slopes[at_rows, pl.ds(D * group, D)] = s + act * (1.0 - s)
            return carry
        lax.fori_loop(0, TILE // 32, step, 0)

    for group, target in ((3, kbuf.at[0]), (1, vbuf.at[0]), (2, qbuf.at[0]), (0, gate_buf)):
        local[group].wait()
        activate(group, target)
    local[4].wait()
    local[5].wait()

    def head_columns(h):
        return pl.ds(pl.multiple_of(h * HEAD_DIM, HEAD_DIM), HEAD_DIM)

    row_ids = lax.broadcasted_iota(jnp.int32, (TILE, TILE), 0)
    col_ids = lax.broadcasted_iota(jnp.int32, (TILE, TILE), 1)

    def weigh(scores, causal):
        z = scores * SCALE
        s = sigmoid(z)
        p = z * s
        slope = s + p * (1.0 - s)
        if causal:
            keep = col_ids <= row_ids
            p = jnp.where(keep, p, 0.0)
            slope = jnp.where(keep, slope, 0.0)
        return p.astype(BF16), slope.astype(BF16)

    def same_forward(h, carry):
        cols = head_columns(h)
        p, slope = weigh(dot_nt(qbuf[0, :, cols], kbuf[0, :, cols]), True)
        p_same[h] = p
        s_same[h] = slope
        mix[:, cols] = dot_nn(p, vbuf[0, :, cols]) * (1.0 / TILE)
        return carry

    def cross_forward(h, carry):
        cols = head_columns(h)
        p, slope = weigh(dot_nt(qbuf[1 - linked, :, cols], kbuf[linked, :, cols]), False)
        p_cross[h] = p
        s_cross[h] = slope
        mix[:, cols] += dot_nn(p, vbuf[linked, :, cols]) * (takes / TILE)
        return carry

    def same_backward(h, carry):
        cols = head_columns(h)
        do = dobuf[0, :, cols]
        ds = (dot_nt(do, vbuf[0, :, cols]) * s_same[h].astype(F32)).astype(BF16)
        s_same[h] = ds
        return carry

    def finish(h, carry):
        cols = head_columns(h)
        do = dobuf[0, :, cols]
        dox = dobuf[1 - linked, :, cols]
        qx, kx, vx = qbuf[1 - linked, :, cols], kbuf[linked, :, cols], vbuf[linked, :, cols]
        ds = s_same[h]
        dsx = (dot_nt(dox, vx) * s_cross[h].astype(F32)).astype(BF16)
        dv = (dot_tn(p_same[h], do) + dot_tn(p_cross[h], dox) * gives) * (1.0 / TILE)
        dk = (dot_tn(ds, qbuf[0, :, cols]) + dot_tn(dsx, qx) * gives) * (SCALE / TILE)
        dq = (dot_nn(ds, kbuf[0, :, cols]) + dot_nn(dsx, kx) * takes) * (SCALE / TILE)
        for i, value in ((1, dv), (2, dq), (3, dk)):
            there = pl.ds(pl.multiple_of(D * i + h * HEAD_DIM, HEAD_DIM), HEAD_DIM)
            grads[:, there] = (value * slopes[:, there]).astype(BF16)
        return carry

    first_axis()
    lax.fori_loop(0, 4, same_forward, 0)
    second_axis(0)
    lax.fori_loop(4, 8, same_forward, 0)
    first_axis_far()
    second_axis(-1)

    for i in range(PIECES):
        for raw, target, number in ((kraw, kbuf, K_IN), (vraw, vbuf, V_IN), (qraw, qbuf, Q_IN)):
            arrived(raw.at[:, columns(i)], number + i)
            value = raw[:, columns(i)].astype(F32)
            target[1, :, columns(i)] = (value * sigmoid(value)).astype(BF16)
        lax.fori_loop(2 * i, 2 * i + 2, cross_forward, 0)

    def norm(i, carry):
        at_rows = pl.ds(pl.multiple_of(i * 32, 32), 32)
        mixed = mix[at_rows, :]
        centered = mixed - jnp.mean(mixed, axis=-1, keepdims=True)
        inv_std = lax.rsqrt(jnp.mean(centered * centered, axis=-1, keepdims=True) + EPSILON)
        normed = centered * inv_std
        live = lax.broadcasted_iota(jnp.int32, (32, 1), 0) + i * 32 < valid
        cot = jnp.where(live, og_v[at_rows, :].astype(F32), 0.0)
        grads[at_rows, pl.ds(0, D)] = (cot * normed * slopes[at_rows, pl.ds(0, D)]).astype(BF16)
        grad_norm = cot * gate_buf[at_rows, :].astype(F32)
        grad_mix = inv_std * (
            grad_norm
            - jnp.mean(grad_norm, axis=-1, keepdims=True)
            - normed * jnp.mean(grad_norm * normed, axis=-1, keepdims=True)
        )
        dobuf[0, at_rows, :] = grad_mix.astype(BF16)
        kraw[at_rows, :] = (grad_mix * takes).astype(BF16)
        return carry

    lax.fori_loop(0, TILE // 32, norm, 0)
    for i in range(PIECES):
        send(kraw.at[:, columns(i)], doraw.at[:, columns(i)], DO_IN + i, before)
    second_axis(1)
    lax.fori_loop(0, 8, same_backward, 0)
    second_axis(2)
    for i in range(PIECES):
        arrived(doraw.at[:, columns(i)], DO_IN + i)
        dobuf[1, :, columns(i)] = doraw[:, columns(i)]
        lax.fori_loop(2 * i, 2 * i + 2, finish, 0)

    for a in LANES:
        second_axis_far(a)
    for a in LANES:
        for b in LANES:
            swapped(a, b)

    def out_copy(i):
        return copy(staged.at[:, columns(i)], out.at[0, :, columns(i)], OUT + i, {"section": mod(section - 1, SECTIONS)})

    for i in range(PIECES):
        weights = wbuf[pl.ds(PIECE * i, PIECE), :]
        staged[:, columns(i)] = dot_nt(grads[...], weights).astype(BF16)

        @pl.when(section > 0)
        def _():
            out_copy(i).start()

    for moved in sent:
        moved.wait_send()

    @pl.when(section > 0)
    def _():
        for i in range(PIECES):
            out_copy(i).wait_send()

    @pl.when(section < SECTIONS - 1)
    def _():
        for i in range(PIECES):
            out_copy(i).wait_recv()

    @pl.when(section == SECTIONS - 1)
    def _():
        mix[...] = jnp.zeros_like(mix)
        kraw[...] = mix[...].astype(BF16)
        zeros = pltpu.make_async_copy(kraw, out.at[0], local_sem.at[0])
        zeros.start()
        zeros.wait()


def body(pre_act, out_grad, proj_weight, lengths, link_bits):
    wide = pltpu.VMEM((TILE, D), BF16)
    pair = pltpu.VMEM((2, TILE, D), BF16)
    scores = pltpu.VMEM((HEADS, TILE, TILE), BF16)
    anywhere = pl.BlockSpec(memory_space=pl.ANY)
    scalars = pl.BlockSpec(memory_space=pltpu.SMEM)
    return pl.pallas_call(
        kernel,
        out_shape=jax.ShapeDtypeStruct((1, TILE, D), BF16),
        in_specs=[scalars, scalars, anywhere, anywhere, anywhere],
        out_specs=anywhere,
        scratch_shapes=[
            pltpu.VMEM((TILE, 4 * D), BF16),
            wide,
            pltpu.VMEM((D, 4 * D), BF16),
            wide, wide, wide, wide,
            pair, pair, pair, pair,
            wide,
            pltpu.VMEM((TILE, 4 * D), F32),
            scores, scores, scores, scores,
            pltpu.VMEM((TILE, D), F32),
            pltpu.VMEM((TILE, 4 * D), BF16),
            wide,
            pltpu.SemaphoreType.DMA((TRANSFERS,)),
            pltpu.SemaphoreType.DMA((TRANSFERS,)),
            pltpu.SemaphoreType.DMA((6,)),
        ],
        compiler_params=pltpu.CompilerParams(
            collective_id=0, has_side_effects=True, vmem_limit_bytes=48 * 1024 * 1024
        ),
    )(lengths, link_bits, pre_act, out_grad, proj_weight)


def solution(mesh):
    placed = (
        P("section", "seq", None),
        P("section", "seq", None),
        P("section", "seq", None),
        P("section", None),
        P("section", "seq"),
    )
    return jax.shard_map(
        body, mesh=mesh, in_specs=placed, out_specs=P("section", "seq", None), check_vma=False
    )
```

time: 117 us -> 75.1 us (0.64)
  the two profiles are of different devices: /device:TPU:1 before, /device:TPU:198 now
where the time goes in v1:
time: 75.1 us; the launch traced here: 74.8 us
  Pallas kernels  69.1 us (92%)
  local copies, waits for them, and re-layouts  5.03 us (7%)
    pallas_call x1, Pallas kernels, body(): pl.pallas_call(kernel, out_shape=jax.ShapeDtypeStruct((1, TILE, D), BF16)...  69.1 us
    unnamed x9, local copies, waits for them, and re-layouts  5.03 us

profile of v1, /device:TPU:198, one launch (start us, length us, event | category | flops | bytes accessed | tf_op | source)
XLA Modules:
  0.0 74.8 jit_solution(11177165553079248575)
XLA Ops:
  0.7 0.0 copy-start
  0.7 1.6 %copy-done = bf16[1,256,4096]{2,1,0:T(8,128)(2,1)S(1)} copy-done((bf16[1,256,4096]{2,1,0:T(8,128)(2,1)S(1)}, bf16[1,256,4096]{2,1,0:T(8,128)(2,1)}, u32[]{:S(2)}) %copy-start) | copy-done | bytes 2097176
  2.2 0.0 copy-start.1
  2.2 1.0 %copy-done.1 = bf16[1,256,1024]{2,1,0:T(8,128)(2,1)S(1)} copy-done((bf16[1,256,1024]{2,1,0:T(8,128)(2,1)S(1)}, bf16[1,256,1024]{2,1,0:T(8,128)(2,1)}, u32[]{:S(2)}) %copy-start.1) | copy-done | bytes 524312
  3.3 0.0 copy-start.2
  3.3 0.9 %copy-done.2 = bf16[1,32,4096]{2,1,0:T(8,128)(2,1)S(1)} copy-done((bf16[1,32,4096]{2,1,0:T(8,128)(2,1)S(1)}, bf16[1,32,4096]{2,1,0:T(8,128)(2,1)}, u32[]{:S(2)}) %copy-start.2) | copy-done | bytes 262168
  4.2 0.0 copy-start.3
  4.2 0.7 copy-done.3
  4.9 69.1 %shard_map.55 = bf16[1,256,1024]{2,1,0:T(8,128)(2,1)S(1)} custom-call(s32[1,32]{1,0:T(1,128)S(1)} %copy-done.3, s32[1,1]{1,0:T(1,128)S(6)} %copy.7.link_ref, bf16[1,256,4096]{2,1,0:T(8,128)(2,1)S(1)} %copy-done, bf16[1,256,1024]{2,1,0:T(8,128)(2,1)S(1)} %copy-done.1, bf16[1,32,4096]{2,1,0:T(8,128)(2,1)S(1)} %copy-done.2), custom_call_target="tpu_custom_call" | custom-call | tf_op jit(solution)/shard_map/pallas_call | solution.py:355
  74.0 0.8 %copy.8 = bf16[1,256,1024]{2,1,0:T(8,128)(2,1)} copy(bf16[1,256,1024]{2,1,0:T(8,128)(2,1)S(1)} %shard_map.55) | data formatting | bytes 1048576
Async XLA Ops:
  0.7 1.6 %copy-start = (bf16[1,256,4096]{2,1,0:T(8,128)(2,1)S(1)}, bf16[1,256,4096]{2,1,0:T(8,128)(2,1)}, u32[]{:S(2)}) copy-start(bf16[1,256,4096]{2,1,0:T(8,128)(2,1)} %pre.1) | copy-start | bytes 6291460
  2.2 1.0 %copy-start.1 = (bf16[1,256,1024]{2,1,0:T(8,128)(2,1)S(1)}, bf16[1,256,1024]{2,1,0:T(8,128)(2,1)}, u32[]{:S(2)}) copy-start(bf16[1,256,1024]{2,1,0:T(8,128)(2,1)} %og.1) | copy-start | bytes 1572868
  3.3 0.9 %copy-start.2 = (bf16[1,32,4096]{2,1,0:T(8,128)(2,1)S(1)}, bf16[1,32,4096]{2,1,0:T(8,128)(2,1)}, u32[]{:S(2)}) copy-start(bf16[1,32,4096]{2,1,0:T(8,128)(2,1)} %w.1) | copy-start | bytes 786436
  4.2 0.7 copy-start.3

commit v2 on v1

v2 whole, which is shorter than its diff:
```python
import jax
import jax.numpy as jnp
from jax import lax
from jax.experimental import pallas as pl
from jax.experimental.pallas import tpu as pltpu
from jax.sharding import PartitionSpec as P

D = 1024
HEADS = 8
HEAD_DIM = 128
TILE = 256
SIDE = 4
SECTIONS = 16
DEVICES = 32
SHARD = D // DEVICES
EPSILON = 1e-05
MESH = pl.DeviceIdType.MESH
F32 = jnp.float32
BF16 = jnp.bfloat16
SCALE = HEAD_DIM ** (-0.5)

CHUNK = 128
PIECE = 512
GROUP = PIECE // HEAD_DIM
UNROLL = 2

STEPS = (0, -1, 1, 2)
TURN = (-1, 1, -1, 1)

A_IN = 0
B_IN = 3
SWAP = 15
Q_IN = 31
O_IN = 35
DO_IN = 39
DQ_IN = 43
OUT = 47
TRANSFERS = 51


def mod(value, size):
    return lax.rem(value + size, size)


def dot_nn(a, b):
    return lax.dot_general(a, b, (((1,), (0,)), ((), ())), preferred_element_type=F32)


def dot_nt(a, b):
    return lax.dot_general(a, b, (((1,), (1,)), ((), ())), preferred_element_type=F32)


def dot_tn(a, b):
    return lax.dot_general(a, b, (((0,), (0,)), ((), ())), preferred_element_type=F32)


def sigmoid(values):
    return 0.5 * jnp.tanh(0.5 * values) + 0.5


def kernel(
    lengths, link_bits, pre, og, w, out,
    len_ref, link_ref, pre_v, og_v, wbuf, kbuf, vbuf, qbuf, gate_buf, slopes,
    qraw, oraw, doraw, dqraw, qx, dobuf, o_stage, do_stage, dq_stage,
    p_same, s_same, p_cross, s_cross, mix, dq_sum, grads, staged,
    send_sem, recv_sem, local_sem,
):
    section = lax.axis_index("section")
    me = lax.axis_index("seq")
    core = lax.rem(me, 2)
    cy = lax.rem(lax.div(me, 2), SIDE)
    cx = lax.div(me, 2 * SIDE)
    other = me + 1 - 2 * core
    after = mod(me + 1, DEVICES)
    before = mod(me - 1, DEVICES)

    def at(a, b):
        x = mod(cx + a * (1 - core) + b * core, SIDE)
        y = mod(cy + a * core + b * (1 - core), SIDE)
        return (x * SIDE + y) * 2 + core

    def block(device):
        return wbuf.at[pl.ds(pl.multiple_of(device * SHARD, SHARD), SHARD)]

    local = [
        pltpu.make_async_copy(pre.at[0, :, pl.ds(D * i, D)], pre_v.at[:, pl.ds(D * i, D)], local_sem.at[i])
        for i in range(4)
    ]
    local.append(pltpu.make_async_copy(og.at[0], og_v, local_sem.at[4]))
    local.append(pltpu.make_async_copy(w.at[0], block(me), local_sem.at[5]))
    local.append(pltpu.make_async_copy(lengths, len_ref, local_sem.at[6]))
    local.append(pltpu.make_async_copy(link_bits, link_ref, local_sem.at[7]))
    barrier = pltpu.get_barrier_semaphore()
    peers = [
        {"seq": other},
        {"seq": at(1, 0)},
        {"seq": at(-1, 0)},
        {"seq": at(0, 1)},
        {"seq": at(0, -1)},
        {"seq": after + (before - after) * (1 - core)},
        {"section": mod(section + 1, SECTIONS)},
        {"section": mod(section - 1, SECTIONS)},
    ]
    for peer in peers:
        pl.semaphore_signal(barrier, inc=1, device_id=peer, device_id_type=MESH)
    for i in (2, 3, 1, 6, 7, 0, 4, 5):
        local[i].start()
    pl.semaphore_wait(barrier, len(peers))

    sent = []

    def copy(src, dst, number, target):
        return pltpu.make_async_remote_copy(
            src_ref=src, dst_ref=dst, send_sem=send_sem.at[number], recv_sem=recv_sem.at[number],
            device_id=target, device_id_type=MESH,
        )

    def send(src, dst, number, target):
        moved = copy(src, dst, number, {"seq": target})
        moved.start()
        sent.append(moved)

    def arrived(dst, number):
        copy(dst, dst, number, {"seq": other}).wait_recv()

    def chunk(r):
        return pl.ds(CHUNK * r, CHUNK)

    def columns(g):
        return pl.ds(PIECE * g, PIECE)

    def piece(ref, r, g):
        return ref.at[chunk(r), columns(g)]

    def swap(src, i, j):
        send(src, block(at(STEPS[i], STEPS[j])), SWAP + 4 * i + j, other)

    def first_out(src):
        send(src, block(me), A_IN, at(1, 0))

    def first_back(src):
        send(src, block(me), A_IN + 1, at(-1, 0))

    def second_out(src, i):
        there = block(at(STEPS[i], 0))
        send(src, there, B_IN + 3 * i, at(0, TURN[i]))
        send(src, there, B_IN + 3 * i + 1, at(0, -TURN[i]))

    def first_near():
        here = block(at(-1, 0))
        arrived(here, A_IN)
        send(here, here, A_IN + 2, at(1, 0))
        second_out(here, 1)
        swap(here, 1, 0)

    def first_behind():
        here = block(at(1, 0))
        arrived(here, A_IN + 1)
        second_out(here, 2)
        swap(here, 2, 0)

    def first_far():
        here = block(at(2, 0))
        arrived(here, A_IN + 2)
        second_out(here, 3)
        swap(here, 3, 0)

    def second_near(i):
        here = block(at(STEPS[i], -TURN[i]))
        arrived(here, B_IN + 3 * i)
        send(here, here, B_IN + 3 * i + 2, at(0, TURN[i]))
        swap(here, i, STEPS.index(-TURN[i]))

    def second_behind(i):
        here = block(at(STEPS[i], TURN[i]))
        arrived(here, B_IN + 3 * i + 1)
        swap(here, i, STEPS.index(TURN[i]))

    def second_far(i):
        here = block(at(STEPS[i], 2))
        arrived(here, B_IN + 3 * i + 2)
        swap(here, i, 3)

    def swapped(i):
        for j in range(4):
            x, y = mod(cx + STEPS[i], SIDE), mod(cy + STEPS[j], SIDE)
            number = SWAP + (4 * j + i) * (1 - core) + (4 * i + j) * core
            arrived(block((x * SIDE + y) * 2 + 1 - core), number)

    def send_q():
        for r in range(2):
            for g in range(2):
                rows = pl.ds(CHUNK * r, CHUNK)
                send(pre.at[0, rows, pl.ds(2 * D + PIECE * g, PIECE)], piece(qraw, r, g), Q_IN + 2 * r + g, before)

    send_q()
    first_out(w.at[0])
    first_back(w.at[0])
    second_out(w.at[0], 0)
    swap(w.at[0], 0, 0)

    def activate(group, target):
        def step(i, carry):
            rows = pl.ds(pl.multiple_of(i * 32, 32), 32)
            value = pre_v[rows, pl.ds(D * group, D)].astype(F32)
            s = sigmoid(value)
            act = value * s
            target[rows, :] = act.astype(BF16)
            slopes[rows, pl.ds(D * group, D)] = s + act * (1.0 - s)
            return carry

        local[group].wait()
        lax.fori_loop(0, TILE // 32, step, 0)

    def head_columns(h):
        return pl.ds(pl.multiple_of(h * HEAD_DIM, HEAD_DIM), HEAD_DIM)

    def weigh(scores, first_row=None):
        z = scores * SCALE
        s = sigmoid(z)
        p = z * s
        slope = s + p * (1.0 - s)
        if first_row is not None:
            row = lax.broadcasted_iota(jnp.int32, scores.shape, 0) + first_row
            keep = lax.broadcasted_iota(jnp.int32, scores.shape, 1) <= row
            p = jnp.where(keep, p, 0.0)
            slope = jnp.where(keep, slope, 0.0)
        return p.astype(BF16), slope.astype(BF16)

    def same_forward(r):
        keys = CHUNK * (r + 1)

        def step(h, carry):
            cols = head_columns(h)
            p, slope = weigh(dot_nt(qbuf[chunk(r), cols], kbuf[0:keys, cols]), CHUNK * r)
            p_same[h, chunk(r), 0:keys] = p
            s_same[h, chunk(r), 0:keys] = slope
            if keys < TILE:
                p_same[h, chunk(r), keys:TILE] = jnp.zeros((CHUNK, TILE - keys), BF16)
                s_same[h, chunk(r), keys:TILE] = jnp.zeros((CHUNK, TILE - keys), BF16)
            mix[chunk(r), cols] = dot_nn(p, vbuf[0:keys, cols]) * (1.0 / TILE)
            return carry

        lax.fori_loop(0, HEADS, step, 0, unroll=UNROLL)

    def cross_forward(r, g):
        arrived(piece(qraw, r, g), Q_IN + 2 * r + g)
        value = qraw[chunk(r), columns(g)].astype(F32)
        qx[chunk(r), columns(g)] = (value * sigmoid(value)).astype(BF16)

        def step(h, carry):
            cols = head_columns(h)
            p, slope = weigh(dot_nt(qx[chunk(r), cols], kbuf[:, cols]))
            p_cross[h, chunk(r), :] = p
            s_cross[h, chunk(r), :] = slope
            o_stage[chunk(r), cols] = (dot_nn(p, vbuf[:, cols]) * (1.0 / TILE)).astype(BF16)
            return carry

        lax.fori_loop(GROUP * g, GROUP * (g + 1), step, 0, unroll=UNROLL)
        send(piece(o_stage, r, g), piece(oraw, r, g), O_IN + 2 * r + g, after)

    def norm(r):
        for g in range(2):
            arrived(piece(oraw, r, g), O_IN + 2 * r + g)

        def step(i, carry):
            start = CHUNK * r + i * 32
            rows = pl.ds(pl.multiple_of(start, 32), 32)
            mixed = mix[rows, :] + oraw[rows, :].astype(F32) * takes
            centered = mixed - jnp.mean(mixed, axis=-1, keepdims=True)
            inv_std = lax.rsqrt(jnp.mean(centered * centered, axis=-1, keepdims=True) + EPSILON)
            normed = centered * inv_std
            live = lax.broadcasted_iota(jnp.int32, (32, 1), 0) + start < valid
            cot = jnp.where(live, og_v[rows, :].astype(F32), 0.0)
            grads[rows, pl.ds(0, D)] = (cot * normed * slopes[rows, pl.ds(0, D)]).astype(BF16)
            grad_norm = cot * gate_buf[rows, :].astype(F32)
            grad_mix = inv_std * (
                grad_norm
                - jnp.mean(grad_norm, axis=-1, keepdims=True)
                - normed * jnp.mean(grad_norm * normed, axis=-1, keepdims=True)
            )
            dobuf[rows, :] = grad_mix.astype(BF16)
            do_stage[rows, :] = (grad_mix * takes).astype(BF16)
            return carry

        lax.fori_loop(0, CHUNK // 32, step, 0, unroll=UNROLL)
        for g in range(2):
            send(piece(do_stage, r, g), piece(doraw, r, g), DO_IN + 2 * r + g, before)

    def same_backward(r):
        keys = CHUNK * (r + 1)

        def step(h, carry):
            cols = head_columns(h)
            dp = dot_nt(dobuf[chunk(r), cols], vbuf[0:keys, cols])
            ds = (dp * s_same[h, chunk(r), 0:keys].astype(F32)).astype(BF16)
            s_same[h, chunk(r), 0:keys] = ds
            dq_sum[chunk(r), cols] = dot_nn(ds, kbuf[0:keys, cols]) * (SCALE / TILE)
            return carry

        lax.fori_loop(0, HEADS, step, 0, unroll=UNROLL)

    def cross_backward(r, g):
        arrived(piece(doraw, r, g), DO_IN + 2 * r + g)

        def step(h, carry):
            cols = head_columns(h)
            dp = dot_nt(doraw[chunk(r), cols], vbuf[:, cols])
            ds = (dp * s_cross[h, chunk(r), :].astype(F32)).astype(BF16)
            s_cross[h, chunk(r), :] = ds
            dq_stage[chunk(r), cols] = (dot_nn(ds, kbuf[:, cols]) * (SCALE / TILE)).astype(BF16)
            return carry

        lax.fori_loop(GROUP * g, GROUP * (g + 1), step, 0, unroll=UNROLL)
        send(piece(dq_stage, r, g), piece(dqraw, r, g), DQ_IN + 2 * r + g, after)

    def finish_kv(g):
        def step(h, carry):
            cols = head_columns(h)
            dv = (dot_tn(p_same[h], dobuf[:, cols]) + dot_tn(p_cross[h], doraw[:, cols])) * (1.0 / TILE)
            dk = (dot_tn(s_same[h], qbuf[:, cols]) + dot_tn(s_cross[h], qx[:, cols])) * (SCALE / TILE)
            for i, value in ((1, dv), (3, dk)):
                there = pl.ds(pl.multiple_of(D * i + h * HEAD_DIM, HEAD_DIM), HEAD_DIM)
                grads[:, there] = (value * slopes[:, there]).astype(BF16)
            return carry

        lax.fori_loop(GROUP * g, GROUP * (g + 1), step, 0, unroll=UNROLL)

    def finish_q(r, g):
        arrived(piece(dqraw, r, g), DQ_IN + 2 * r + g)
        there = pl.ds(2 * D + PIECE * g, PIECE)
        dq = dq_sum[chunk(r), columns(g)] + dqraw[chunk(r), columns(g)].astype(F32)
        grads[chunk(r), there] = (dq * slopes[chunk(r), there]).astype(BF16)

    def out_copy(i):
        cols = pl.ds(pl.multiple_of(mod(cx + STEPS[i], SIDE) * TILE, TILE), TILE)
        return copy(staged.at[i], out.at[0, :, cols], OUT + i, {"section": mod(section - 1, SECTIONS)})

    def project(i):
        rows = pl.ds(pl.multiple_of(mod(cx + STEPS[i], SIDE) * TILE, TILE), TILE)
        staged[i] = dot_nt(grads[...], wbuf[rows, :]).astype(BF16)

        @pl.when(section > 0)
        def _():
            out_copy(i).start()

    activate(2, qbuf)
    activate(3, kbuf)
    activate(1, vbuf)
    same_forward(0)
    first_near()
    cross_forward(0, 0)
    cross_forward(0, 1)
    first_behind()

    local[6].wait()
    local[7].wait()
    end = jnp.int32(0)
    place = jnp.int32(0)
    total = jnp.int32(0)
    for user in range(DEVICES):
        length = len_ref[0, user]
        begin = end
        end = begin + lax.div(length + (TILE - 1), TILE)
        mine = jnp.logical_and(begin <= me, me < end)
        place = jnp.where(mine, me - begin, place)
        total = jnp.where(mine, length, total)
    valid = jnp.minimum(total - place * TILE, TILE)
    linked = jnp.where(jnp.logical_and(place >= 1, link_ref[0, 0] == 1), 1, 0).astype(jnp.int32)
    takes = linked.astype(F32)

    same_forward(1)
    cross_forward(1, 0)
    cross_forward(1, 1)
    first_far()
    second_near(0)
    activate(0, gate_buf)
    local[4].wait()
    local[5].wait()
    norm(0)
    second_behind(0)
    norm(1)
    second_near(1)
    same_backward(0)
    second_behind(1)
    cross_backward(0, 0)
    cross_backward(0, 1)
    second_near(2)
    same_backward(1)
    second_behind(2)
    cross_backward(1, 0)
    cross_backward(1, 1)
    second_near(3)
    finish_kv(0)
    finish_kv(1)
    for r in range(2):
        for g in range(2):
            finish_q(r, g)
    second_behind(3)
    for i in range(4):
        second_far(i)
        swapped(i)
        project(i)

    for moved in sent:
        moved.wait_send()

    @pl.when(section > 0)
    def _():
        for i in range(4):
            out_copy(i).wait_send()

    @pl.when(section < SECTIONS - 1)
    def _():
        for i in range(4):
            out_copy(i).wait_recv()

    @pl.when(section == SECTIONS - 1)
    def _():
        mix[...] = jnp.zeros_like(mix)
        o_stage[...] = mix[...].astype(BF16)
        zeros = pltpu.make_async_copy(o_stage, out.at[0], local_sem.at[0])
        zeros.start()
        zeros.wait()


def body(pre_act, out_grad, proj_weight, lengths, link_bits):
    wide = pltpu.VMEM((TILE, D), BF16)
    all_columns = pltpu.VMEM((TILE, 4 * D), BF16)
    totals = pltpu.VMEM((TILE, D), F32)
    scores = pltpu.VMEM((HEADS, TILE, TILE), BF16)
    hbm = pl.BlockSpec(memory_space=pltpu.HBM)
    return pl.pallas_call(
        kernel,
        out_shape=jax.ShapeDtypeStruct((1, TILE, D), BF16),
        in_specs=[hbm] * 5,
        out_specs=hbm,
        scratch_shapes=[
            pltpu.SMEM((1, DEVICES), jnp.int32),
            pltpu.SMEM((1, 1), jnp.int32),
            all_columns,
            wide,
            pltpu.VMEM((D, 4 * D), BF16),
            wide, wide, wide, wide,
            pltpu.VMEM((TILE, 4 * D), F32),
            wide, wide, wide, wide, wide, wide, wide, wide, wide,
            scores, scores, scores, scores,
            totals, totals,
            all_columns,
            pltpu.VMEM((SIDE, TILE, TILE), BF16),
            pltpu.SemaphoreType.DMA((TRANSFERS,)),
            pltpu.SemaphoreType.DMA((TRANSFERS,)),
            pltpu.SemaphoreType.DMA((8,)),
        ],
        compiler_params=pltpu.CompilerParams(
            collective_id=0, has_side_effects=True, vmem_limit_bytes=63 * 1024 * 1024
        ),
    )(lengths, link_bits, pre_act, out_grad, proj_weight)


def solution(mesh):
    placed = (
        P("section", "seq", None),
        P("section", "seq", None),
        P("section", "seq", None),
        P("section", None),
        P("section", "seq"),
    )
    return jax.shard_map(
        body, mesh=mesh, in_specs=placed, out_specs=P("section", "seq", None), check_vma=False
    )
```

time: 75.1 us -> 64.8 us (0.86)
  the two profiles are of different devices: /device:TPU:198 before, /device:TPU:1 now
where the time goes in v2:
time: 64.8 us; the launch traced here: 64.3 us
  Pallas kernels  61.7 us (95%)
  local copies, waits for them, and re-layouts  1.87 us (3%)
  between operations  0.66 us (1%)
    pallas_call x1, Pallas kernels, body(): pl.pallas_call(kernel, out_shape=jax.ShapeDtypeStruct((1, TILE, D), BF16)...  61.7 us
    unnamed x1, local copies, waits for them, and re-layouts  1.87 us

profile of v2, /device:TPU:1, one launch (start us, length us, event | category | flops | bytes accessed | tf_op | source)
XLA Modules:
  0.0 64.3 jit_solution(12290335985929139415)
XLA Ops:
  0.7 61.7 %shard_map.55 = bf16[1,256,1024]{2,1,0:T(8,128)(2,1)} custom-call(s32[1,32]{1,0:T(1,128)} %lengths.1, s32[1,1]{1,0:T(1,128)S(6)} %copy.7.link_bits, bf16[1,256,4096]{2,1,0:T(8,128)(2,1)} %pre.1, bf16[1,256,1024]{2,1,0:T(8,128)(2,1)} %og.1, bf16[1,32,4096]{2,1,0:T(8,128)(2,1)} %w.1), custom_call_target="tpu_custom_call" | custom-call | tf_op jit(solution)/shard_map/pallas_call | solution.py:433
  62.4 1.9 %copy.8 = bf16[1,256,1024]{2,1,0:T(8,128)(2,1)} copy(bf16[1,256,1024]{2,1,0:T(8,128)(2,1)} %shard_map.55) | data formatting | bytes 1048576

commit v3 on v2

--- a/solution.py
+++ b/solution.py
@@ -22,7 +22,7 @@
 CHUNK = 128
 PIECE = 512
 GROUP = PIECE // HEAD_DIM
-UNROLL = 2
+UNROLL = 4
 
 STEPS = (0, -1, 1, 2)
 TURN = (-1, 1, -1, 1)
@@ -432,9 +432,9 @@
     hbm = pl.BlockSpec(memory_space=pltpu.HBM)
     return pl.pallas_call(
         kernel,
-        out_shape=jax.ShapeDtypeStruct((1, TILE, D), BF16),
+        out_shape=pltpu.VMEM((1, TILE, D), BF16),
         in_specs=[hbm] * 5,
-        out_specs=hbm,
+        out_specs=pl.BlockSpec(memory_space=pl.ANY),
         scratch_shapes=[
             pltpu.SMEM((1, DEVICES), jnp.int32),
             pltpu.SMEM((1, 1), jnp.int32),

time: 64.8 us -> 62.9 us (0.971)
  the two profiles are of different devices: /device:TPU:1 before, /device:TPU:225 now
where the time goes in v3:
time: 62.9 us; the launch traced here: 62.8 us
  Pallas kernels  61.3 us (97%)
  local copies, waits for them, and re-layouts  0.8 us (1%)
  between operations  0.66 us (1%)
    pallas_call x1, Pallas kernels, body(): pl.pallas_call(kernel, out_shape=pltpu.VMEM((1, TILE, D), BF16), in_specs...  61.3 us

profile of v3, /device:TPU:225, one launch (start us, length us, event | category | flops | bytes accessed | tf_op | source)
XLA Modules:
  0.0 62.8 jit_solution(7925286665637670162)
XLA Ops:
  0.7 61.3 %shard_map.55 = bf16[1,256,1024]{2,1,0:T(8,128)(2,1)S(1)} custom-call(s32[1,32]{1,0:T(1,128)} %lengths.1, s32[1,1]{1,0:T(1,128)S(6)} %copy.8.link_bits, bf16[1,256,4096]{2,1,0:T(8,128)(2,1)} %pre.1, bf16[1,256,1024]{2,1,0:T(8,128)(2,1)} %og.1, bf16[1,32,4096]{2,1,0:T(8,128)(2,1)} %w.1), custom_call_target="tpu_custom_call" | custom-call | tf_op jit(solution)/shard_map/pallas_call | solution.py:433
  62.0 0.8 %copy.7 = bf16[1,256,1024]{2,1,0:T(8,128)(2,1)} copy(bf16[1,256,1024]{2,1,0:T(8,128)(2,1)S(1)} %shard_map.55) | data formatting | bytes 1048576

commit v4 on v3

--- a/solution.py
+++ b/solution.py
@@ -35,7 +35,7 @@
 DO_IN = 39
 DQ_IN = 43
 OUT = 47
-TRANSFERS = 51
+TRANSFERS = 52
 
 
 def mod(value, size):
@@ -118,7 +118,7 @@
     def send(src, dst, number, target):
         moved = copy(src, dst, number, {"seq": target})
         moved.start()
-        sent.append(moved)
+        sent.append(number)
 
     def arrived(dst, number):
         copy(dst, dst, number, {"seq": other}).wait_recv()
@@ -135,34 +135,34 @@
     def swap(src, i, j):
         send(src, block(at(STEPS[i], STEPS[j])), SWAP + 4 * i + j, other)
 
-    def first_out(src):
-        send(src, block(me), A_IN, at(1, 0))
-
-    def first_back(src):
-        send(src, block(me), A_IN + 1, at(-1, 0))
-
-    def second_out(src, i):
-        there = block(at(STEPS[i], 0))
+    def first_out():
+        send(w.at[0], block(me), A_IN, at(1, 0))
+
+    def first_back():
+        send(w.at[0], block(me), A_IN + 1, at(-1, 0))
+
+    def along(i):
+        src, there = w.at[0] if i == 0 else block(at(STEPS[i], 0)), block(at(STEPS[i], 0))
         send(src, there, B_IN + 3 * i, at(0, TURN[i]))
+
+    def against(i):
+        src, there = w.at[0] if i == 0 else block(at(STEPS[i], 0)), block(at(STEPS[i], 0))
         send(src, there, B_IN + 3 * i + 1, at(0, -TURN[i]))
 
     def first_near():
         here = block(at(-1, 0))
         arrived(here, A_IN)
         send(here, here, A_IN + 2, at(1, 0))
-        second_out(here, 1)
         swap(here, 1, 0)
 
     def first_behind():
         here = block(at(1, 0))
         arrived(here, A_IN + 1)
-        second_out(here, 2)
         swap(here, 2, 0)
 
     def first_far():
         here = block(at(2, 0))
         arrived(here, A_IN + 2)
-        second_out(here, 3)
         swap(here, 3, 0)
 
     def second_near(i):
@@ -181,9 +181,10 @@
         arrived(here, B_IN + 3 * i + 2)
         swap(here, i, 3)
 
-    def swapped(i):
-        for j in range(4):
-            x, y = mod(cx + STEPS[i], SIDE), mod(cy + STEPS[j], SIDE)
+    def swapped(i, ys=STEPS):
+        for step in ys:
+            j = STEPS.index(step) if isinstance(step, int) else 1 + lax.div(step + 1, 2)
+            x, y = mod(cx + STEPS[i], SIDE), mod(cy + step, SIDE)
             number = SWAP + (4 * j + i) * (1 - core) + (4 * i + j) * core
             arrived(block((x * SIDE + y) * 2 + 1 - core), number)
 
@@ -194,10 +195,11 @@
                 send(pre.at[0, rows, pl.ds(2 * D + PIECE * g, PIECE)], piece(qraw, r, g), Q_IN + 2 * r + g, before)
 
     send_q()
-    first_out(w.at[0])
-    first_back(w.at[0])
-    second_out(w.at[0], 0)
+    first_out()
+    first_back()
     swap(w.at[0], 0, 0)
+    along(0)
+    against(0)
 
     def activate(group, target):
         def step(i, carry):
@@ -332,9 +334,14 @@
         dq = dq_sum[chunk(r), columns(g)] + dqraw[chunk(r), columns(g)].astype(F32)
         grads[chunk(r), there] = (dq * slopes[chunk(r), there]).astype(BF16)
 
-    def out_copy(i):
-        cols = pl.ds(pl.multiple_of(mod(cx + STEPS[i], SIDE) * TILE, TILE), TILE)
-        return copy(staged.at[i], out.at[0, :, cols], OUT + i, {"section": mod(section - 1, SECTIONS)})
+    def out_copy(i, half=None, number_of=0):
+        start, size = mod(cx + STEPS[i], SIDE) * TILE, TILE
+        src, number = staged.at[i], OUT + i
+        if half is not None:
+            start, size = start + half * CHUNK, CHUNK
+            src, number = staged.at[i, :, pl.ds(pl.multiple_of(half * CHUNK, CHUNK), CHUNK)], OUT + i + number_of
+        cols = pl.ds(pl.multiple_of(start, CHUNK), size)
+        return copy(src, out.at[0, :, cols], number, {"section": mod(section - 1, SECTIONS)})
 
     def project(i):
         rows = pl.ds(pl.multiple_of(mod(cx + STEPS[i], SIDE) * TILE, TILE), TILE)
@@ -343,15 +350,32 @@
         @pl.when(section > 0)
         def _():
             out_copy(i).start()
+
+    near_half = lax.div(cy, 2)
+    beside = 1 - 2 * lax.rem(cy, 2)
+
+    def project_half(half, number_of):
+        start = mod(cx + STEPS[3], SIDE) * TILE + half * CHUNK
+        rows = pl.ds(pl.multiple_of(start, CHUNK), CHUNK)
+        cols = pl.ds(pl.multiple_of(half * CHUNK, CHUNK), CHUNK)
+        staged[3, :, cols] = dot_nt(grads[...], wbuf[rows, :]).astype(BF16)
+
+        @pl.when(section > 0)
+        def _():
+            out_copy(3, half, number_of).start()
 
     activate(2, qbuf)
     activate(3, kbuf)
     activate(1, vbuf)
     same_forward(0)
     first_near()
+    along(1)
+    against(1)
     cross_forward(0, 0)
     cross_forward(0, 1)
     first_behind()
+    along(2)
+    against(2)
 
     local[6].wait()
     local[7].wait()
@@ -373,6 +397,8 @@
     cross_forward(1, 0)
     cross_forward(1, 1)
     first_far()
+    along(3)
+    against(3)
     second_near(0)
     activate(0, gate_buf)
     local[4].wait()
@@ -391,29 +417,41 @@
     cross_backward(1, 0)
     cross_backward(1, 1)
     second_near(3)
+    second_far(0)
     finish_kv(0)
     finish_kv(1)
+    second_far(1)
     for r in range(2):
         for g in range(2):
             finish_q(r, g)
     second_behind(3)
-    for i in range(4):
-        second_far(i)
+    second_far(2)
+    for i in range(3):
         swapped(i)
         project(i)
-
-    for moved in sent:
-        moved.wait_send()
+    swapped(3, (0, beside))
+    project_half(near_half, 0)
+    second_far(3)
+    swapped(3, (-beside, 2))
+    project_half(1 - near_half, 1)
+
+    for number in sent:
+        moved = piece(o_stage, 0, 0) if number >= Q_IN else block(0)
+        copy(moved, moved, number, {"seq": other}).wait_send()
 
     @pl.when(section > 0)
     def _():
-        for i in range(4):
+        for i in range(3):
             out_copy(i).wait_send()
+        out_copy(3, near_half, 0).wait_send()
+        out_copy(3, 1 - near_half, 1).wait_send()
 
     @pl.when(section < SECTIONS - 1)
     def _():
-        for i in range(4):
+        for i in range(3):
             out_copy(i).wait_recv()
+        out_copy(3, near_half, 0).wait_recv()
+        out_copy(3, 1 - near_half, 1).wait_recv()
 
     @pl.when(section == SECTIONS - 1)
     def _():

time: 62.9 us -> 61.2 us (0.973)
  the two profiles are of different devices: /device:TPU:225 before, /device:TPU:1 now
where the time goes in v4:
time: 61.2 us; the launch traced here: 61.1 us
  Pallas kernels  59.6 us (97%)
  local copies, waits for them, and re-layouts  0.8 us (1%)
  between operations  0.66 us (1%)
    pallas_call x1, Pallas kernels, body(): pl.pallas_call(kernel, out_shape=pltpu.VMEM((1, TILE, D), BF16), in_specs...  59.6 us

profile of v4, /device:TPU:1, one launch (start us, length us, event | category | flops | bytes accessed | tf_op | source)
XLA Modules:
  0.0 61.1 jit_solution(12280346491519510186)
XLA Ops:
  0.7 59.6 %shard_map.55 = bf16[1,256,1024]{2,1,0:T(8,128)(2,1)S(1)} custom-call(s32[1,32]{1,0:T(1,128)} %lengths.1, s32[1,1]{1,0:T(1,128)S(6)} %copy.8.link_bits, bf16[1,256,4096]{2,1,0:T(8,128)(2,1)} %pre.1, bf16[1,256,1024]{2,1,0:T(8,128)(2,1)} %og.1, bf16[1,32,4096]{2,1,0:T(8,128)(2,1)} %w.1), custom_call_target="tpu_custom_call" | custom-call | tf_op jit(solution)/shard_map/pallas_call | solution.py:471
  60.3 0.8 %copy.7 = bf16[1,256,1024]{2,1,0:T(8,128)(2,1)} copy(bf16[1,256,1024]{2,1,0:T(8,128)(2,1)S(1)} %shard_map.55) | data formatting | bytes 1048576

commit v5 on v4

--- a/solution.py
+++ b/solution.py
@@ -418,14 +418,14 @@
     cross_backward(1, 1)
     second_near(3)
     second_far(0)
+    second_far(1)
     finish_kv(0)
     finish_kv(1)
-    second_far(1)
+    second_behind(3)
+    second_far(2)
     for r in range(2):
         for g in range(2):
             finish_q(r, g)
-    second_behind(3)
-    second_far(2)
     for i in range(3):
         swapped(i)
         project(i)

time: 61.2 us -> 61.2 us (level)
  no operation moved by 1% of the time
where the time goes in v5:
time: 61.2 us; the launch traced here: 61.1 us
  Pallas kernels  59.6 us (97%)
  local copies, waits for them, and re-layouts  0.8 us (1%)
  between operations  0.66 us (1%)
    pallas_call x1, Pallas kernels, body(): pl.pallas_call(kernel, out_shape=pltpu.VMEM((1, TILE, D), BF16), in_specs...  59.6 us

profile of v5, /device:TPU:1, one launch (start us, length us, event | category | flops | bytes accessed | tf_op | source)
XLA Modules:
  0.0 61.1 jit_solution(11031438238672290224)
XLA Ops:
  0.7 59.6 %shard_map.55 = bf16[1,256,1024]{2,1,0:T(8,128)(2,1)S(1)} custom-call(s32[1,32]{1,0:T(1,128)} %lengths.1, s32[1,1]{1,0:T(1,128)S(6)} %copy.8.link_bits, bf16[1,256,4096]{2,1,0:T(8,128)(2,1)} %pre.1, bf16[1,256,1024]{2,1,0:T(8,128)(2,1)} %og.1, bf16[1,32,4096]{2,1,0:T(8,128)(2,1)} %w.1), custom_call_target="tpu_custom_call" | custom-call | tf_op jit(solution)/shard_map/pallas_call | solution.py:471
  60.3 0.8 %copy.7 = bf16[1,256,1024]{2,1,0:T(8,128)(2,1)} copy(bf16[1,256,1024]{2,1,0:T(8,128)(2,1)S(1)} %shard_map.55) | data formatting | bytes 1048576
